TPU v7x, 32 devices: a whole 2x2x4 slice. The times are simulated.
32 devices in a mesh: grp: 4 (over x, core), mem: 8 (over z, y).
Axes of the slice: x: 2, y: 2, z: 4, core: 2. Of those that a mesh axis runs over, the one named last changes fastest.
Arguments:
- amplitudes: bfloat16 [8, 8, 128, 2048], P('mem', 'grp'), may hold values from -6 to 6
- integrals: bfloat16 [8, 8, 2048, 2048], P('mem', 'grp'), may hold values from -0.0625 to 0.0625
- triples: int32 [4, 8, 12], P('grp', 'mem'), may hold values from -1 to 15, as said below
Outputs:
- residual: bfloat16 [8, 8, 128, 2048], P('grp', 'mem')
Inputs may be any that keep to these rules, and one draw needn't show every extreme that they name: On each device the live codes are distinct, increasing, and stand before the empty slots; one device lists exactly 12 triples, the others 12, 6, 3 or 1.
All inputs are finite; a program needn't handle non-finite values.
Results may differ from a plain program's by a relative error of at most 0.001.
Values may be sent and summed in bfloat16 or wider, within the bound.
A program may use at most 128 MiB of HBM per device.

v0:
```python
import jax
import jax.numpy as jnp
from jax import lax
from jax.sharding import PartitionSpec as P


def body(amplitudes, integrals, triples):
    occ_local, cd_local, rows, width = amplitudes.shape
    ab_local = integrals.shape[0]
    gathered = lax.all_gather(amplitudes, "mem", axis=0, tiled=True)
    occ_tiles = gathered.shape[0]
    pairs = ab_local * cd_local
    codes = triples.reshape(-1)
    capacity = codes.shape[0]
    live = codes >= 0
    safe = jnp.maximum(codes, 0)
    occ_index = jnp.where(live, safe // pairs, occ_tiles)
    ab_index = safe % pairs // cd_local
    cd_index = safe % cd_local
    amp_flat = gathered.reshape(occ_tiles * cd_local, rows, width)
    int_flat = integrals.reshape(pairs, width, width)
    live_count = jnp.sum(live.astype(jnp.int32))
    empty = jnp.zeros((occ_tiles * ab_local, rows, width), jnp.float32)

    def one_triple(slot, total):
        place = jnp.minimum(slot, capacity - 1)
        occ = occ_index[place]
        outer = ab_index[place]
        inner = cd_index[place]
        left = lax.dynamic_index_in_dim(amp_flat, occ * cd_local + inner, 0, keepdims=False)
        right = lax.dynamic_index_in_dim(int_flat, outer * cd_local + inner, 0, keepdims=False)
        product = lax.dot_general(
            left, right, (((1,), (1,)), ((), ())), preferred_element_type=jnp.float32
        )
        target_row = (occ - 0) * ab_local + outer
        current = lax.dynamic_index_in_dim(total, target_row, 0, keepdims=False)
        return lax.dynamic_update_index_in_dim(total, current + product, target_row, 0)

    partial_value = lax.fori_loop(0, live_count, one_triple, empty)
    summed = lax.psum_scatter(
        partial_value.reshape(occ_tiles, ab_local, rows, width),
        "grp",
        scatter_dimension=0,
        tiled=True,
    )
    return summed.astype(jnp.bfloat16)


def solution(mesh):
    return jax.shard_map(
        body,
        mesh=mesh,
        in_specs=(P("mem", "grp", None, None), P("mem", "grp", None, None), P("grp", "mem", None)),
        out_specs=P("grp", "mem", None, None),
        check_vma=False,
    )
```

profile of v0, /device:TPU:2, one launch (start us, length us, event | category | flops | bytes accessed | tf_op | source)
XLA Modules:
  0.0 398.6 jit_solution(8352486620878535622)
XLA Ops:
  6.5 0.7 all-gather.2.cloned.1.call-update
  7.3 1.3 and_select_fusion
  8.6 127.1 %all-gather.2.cloned.1.call-done = bf16[8,2,128,2048]{3,2,1,0:T(8,128)(2,1)} async-done(((bf16[1,2,128,2048]{3,2,1,0:T(8,128)(2,1)}), bf16[8,2,128,2048]{3,2,1,0:T(8,128)(2,1)}) %all-gather.2.cloned.1.call-update) | async-done | bytes 8388624 | tf_op jit(solution)/shard_map/all_gather | solution.py:10
  135.7 4.3 %broadcast_in_dim.11 = f32[8,128,2048]{2,1,0:T(8,128)} broadcast(f32[]{:T(128)} %constant.71.clone.1), dimensions={} | broadcast | bytes 8388612 | tf_op jit(solution)/shard_map/broadcast_in_dim | solution.py:23
  140.0 180.6 %while.10 = (s32[]{:T(128)}, f32[8,128,2048]{2,1,0:T(8,128)}, s32[]{:T(128)}, s32[12]{0:T(128)S(1)}, s32[12]{0:T(128)S(1)}, /*index=5*/s32[12]{0:T(128)S(1)}, bf...) while((s32[]{:T(128)}, f32[8,128,2048]{2,1,0:T(8,128)}, ...), condition=%wide.region_2.3_spmd, body=%wide.region_1.2_spmd.sunk | while | flops 1074003968 | bytes 13107609 | solution.py:39
  140.6 0.6 dynamic_slice.45
  144.3 0.6 dynamic_slice.47
  146.2 1.3 constant_dynamic-slice_fusion.2
  147.5 7.5 %fusion.22 = f32[8,128,2048]{2,1,0:T(8,128)} fusion(f32[8,128,2048]{2,1,0:T(8,128)} %get-tuple-element.136, s32[]{:T(128)S(6)} %select_n.56, bf16[2,2048,2048]{2,1,0:T(8,128)(2,1)} %get-tuple-element.158, s32[]{:T(128)S(6)} %select_n.57, f32[1,128,2048]{2,1,0:T(8,128)S(1)} %constant_dynamic-slice_fusion.2, ...), kind=kOutput, calls=%fused_computation.5.clone.1 | convolution fusion | flops 1074003968 | bytes 11010060 | tf_op jit(solution)/shard_map/while/body/dot_general | solution.py:32
  155.7 0.6 dynamic_slice.45
  159.3 0.6 dynamic_slice.47
  161.2 1.3 constant_dynamic-slice_fusion.2
  162.5 7.5 %fusion.22 = f32[8,128,2048]{2,1,0:T(8,128)} fusion(f32[8,128,2048]{2,1,0:T(8,128)} %get-tuple-element.136, s32[]{:T(128)S(6)} %select_n.56, bf16[2,2048,2048]{2,1,0:T(8,128)(2,1)} %get-tuple-element.158, s32[]{:T(128)S(6)} %select_n.57, f32[1,128,2048]{2,1,0:T(8,128)S(1)} %constant_dynamic-slice_fusion.2, ...), kind=kOutput, calls=%fused_computation.5.clone.1 | convolution fusion | flops 1074003968 | bytes 11010060 | tf_op jit(solution)/shard_map/while/body/dot_general | solution.py:32
  170.7 0.6 dynamic_slice.45
  171.9 0.6 dynamic_slice.46
  174.4 0.6 dynamic_slice.47
  176.3 1.3 constant_dynamic-slice_fusion.2
  177.6 7.5 %fusion.22 = f32[8,128,2048]{2,1,0:T(8,128)} fusion(f32[8,128,2048]{2,1,0:T(8,128)} %get-tuple-element.136, s32[]{:T(128)S(6)} %select_n.56, bf16[2,2048,2048]{2,1,0:T(8,128)(2,1)} %get-tuple-element.158, s32[]{:T(128)S(6)} %select_n.57, f32[1,128,2048]{2,1,0:T(8,128)S(1)} %constant_dynamic-slice_fusion.2, ...), kind=kOutput, calls=%fused_computation.5.clone.1 | convolution fusion | flops 1074003968 | bytes 11010060 | tf_op jit(solution)/shard_map/while/body/dot_general | solution.py:32
  185.7 0.6 dynamic_slice.45
  191.2 1.3 constant_dynamic-slice_fusion.2
  192.5 7.5 %fusion.22 = f32[8,128,2048]{2,1,0:T(8,128)} fusion(f32[8,128,2048]{2,1,0:T(8,128)} %get-tuple-element.136, s32[]{:T(128)S(6)} %select_n.56, bf16[2,2048,2048]{2,1,0:T(8,128)(2,1)} %get-tuple-element.158, s32[]{:T(128)S(6)} %select_n.57, f32[1,128,2048]{2,1,0:T(8,128)S(1)} %constant_dynamic-slice_fusion.2, ...), kind=kOutput, calls=%fused_computation.5.clone.1 | convolution fusion | flops 1074003968 | bytes 11010060 | tf_op jit(solution)/shard_map/while/body/dot_general | solution.py:32
  200.6 0.6 dynamic_slice.45
  204.3 0.6 dynamic_slice.47
  206.2 1.3 constant_dynamic-slice_fusion.2
  207.5 7.5 %fusion.22 = f32[8,128,2048]{2,1,0:T(8,128)} fusion(f32[8,128,2048]{2,1,0:T(8,128)} %get-tuple-element.136, s32[]{:T(128)S(6)} %select_n.56, bf16[2,2048,2048]{2,1,0:T(8,128)(2,1)} %get-tuple-element.158, s32[]{:T(128)S(6)} %select_n.57, f32[1,128,2048]{2,1,0:T(8,128)S(1)} %constant_dynamic-slice_fusion.2, ...), kind=kOutput, calls=%fused_computation.5.clone.1 | convolution fusion | flops 1074003968 | bytes 11010060 | tf_op jit(solution)/shard_map/while/body/dot_general | solution.py:32
  215.6 0.6 dynamic_slice.45
  221.1 1.3 constant_dynamic-slice_fusion.2
  222.5 7.5 %fusion.22 = f32[8,128,2048]{2,1,0:T(8,128)} fusion(f32[8,128,2048]{2,1,0:T(8,128)} %get-tuple-element.136, s32[]{:T(128)S(6)} %select_n.56, bf16[2,2048,2048]{2,1,0:T(8,128)(2,1)} %get-tuple-element.158, s32[]{:T(128)S(6)} %select_n.57, f32[1,128,2048]{2,1,0:T(8,128)S(1)} %constant_dynamic-slice_fusion.2, ...), kind=kOutput, calls=%fused_computation.5.clone.1 | convolution fusion | flops 1074003968 | bytes 11010060 | tf_op jit(solution)/shard_map/while/body/dot_general | solution.py:32
  230.6 0.6 dynamic_slice.45
  236.1 1.3 constant_dynamic-slice_fusion.2
  237.4 7.5 %fusion.22 = f32[8,128,2048]{2,1,0:T(8,128)} fusion(f32[8,128,2048]{2,1,0:T(8,128)} %get-tuple-element.136, s32[]{:T(128)S(6)} %select_n.56, bf16[2,2048,2048]{2,1,0:T(8,128)(2,1)} %get-tuple-element.158, s32[]{:T(128)S(6)} %select_n.57, f32[1,128,2048]{2,1,0:T(8,128)S(1)} %constant_dynamic-slice_fusion.2, ...), kind=kOutput, calls=%fused_computation.5.clone.1 | convolution fusion | flops 1074003968 | bytes 11010060 | tf_op jit(solution)/shard_map/while/body/dot_general | solution.py:32
  245.6 0.6 dynamic_slice.45
  251.1 1.3 constant_dynamic-slice_fusion.2
  252.4 7.5 %fusion.22 = f32[8,128,2048]{2,1,0:T(8,128)} fusion(f32[8,128,2048]{2,1,0:T(8,128)} %get-tuple-element.136, s32[]{:T(128)S(6)} %select_n.56, bf16[2,2048,2048]{2,1,0:T(8,128)(2,1)} %get-tuple-element.158, s32[]{:T(128)S(6)} %select_n.57, f32[1,128,2048]{2,1,0:T(8,128)S(1)} %constant_dynamic-slice_fusion.2, ...), kind=kOutput, calls=%fused_computation.5.clone.1 | convolution fusion | flops 1074003968 | bytes 11010060 | tf_op jit(solution)/shard_map/while/body/dot_general | solution.py:32
  260.5 0.6 dynamic_slice.45
  266.1 1.3 constant_dynamic-slice_fusion.2
  267.4 7.5 %fusion.22 = f32[8,128,2048]{2,1,0:T(8,128)} fusion(f32[8,128,2048]{2,1,0:T(8,128)} %get-tuple-element.136, s32[]{:T(128)S(6)} %select_n.56, bf16[2,2048,2048]{2,1,0:T(8,128)(2,1)} %get-tuple-element.158, s32[]{:T(128)S(6)} %select_n.57, f32[1,128,2048]{2,1,0:T(8,128)S(1)} %constant_dynamic-slice_fusion.2, ...), kind=kOutput, calls=%fused_computation.5.clone.1 | convolution fusion | flops 1074003968 | bytes 11010060 | tf_op jit(solution)/shard_map/while/body/dot_general | solution.py:32
  275.6 0.6 dynamic_slice.45
  281.1 1.3 constant_dynamic-slice_fusion.2
  282.4 7.5 %fusion.22 = f32[8,128,2048]{2,1,0:T(8,128)} fusion(f32[8,128,2048]{2,1,0:T(8,128)} %get-tuple-element.136, s32[]{:T(128)S(6)} %select_n.56, bf16[2,2048,2048]{2,1,0:T(8,128)(2,1)} %get-tuple-element.158, s32[]{:T(128)S(6)} %select_n.57, f32[1,128,2048]{2,1,0:T(8,128)S(1)} %constant_dynamic-slice_fusion.2, ...), kind=kOutput, calls=%fused_computation.5.clone.1 | convolution fusion | flops 1074003968 | bytes 11010060 | tf_op jit(solution)/shard_map/while/body/dot_general | solution.py:32
  290.6 0.6 dynamic_slice.45
  296.1 1.3 constant_dynamic-slice_fusion.2
  297.5 7.5 %fusion.22 = f32[8,128,2048]{2,1,0:T(8,128)} fusion(f32[8,128,2048]{2,1,0:T(8,128)} %get-tuple-element.136, s32[]{:T(128)S(6)} %select_n.56, bf16[2,2048,2048]{2,1,0:T(8,128)(2,1)} %get-tuple-element.158, s32[]{:T(128)S(6)} %select_n.57, f32[1,128,2048]{2,1,0:T(8,128)S(1)} %constant_dynamic-slice_fusion.2, ...), kind=kOutput, calls=%fused_computation.5.clone.1 | convolution fusion | flops 1074003968 | bytes 11010060 | tf_op jit(solution)/shard_map/while/body/dot_general | solution.py:32
  305.6 0.6 dynamic_slice.45
  311.1 1.3 constant_dynamic-slice_fusion.2
  312.5 7.5 %fusion.22 = f32[8,128,2048]{2,1,0:T(8,128)} fusion(f32[8,128,2048]{2,1,0:T(8,128)} %get-tuple-element.136, s32[]{:T(128)S(6)} %select_n.56, bf16[2,2048,2048]{2,1,0:T(8,128)(2,1)} %get-tuple-element.158, s32[]{:T(128)S(6)} %select_n.57, f32[1,128,2048]{2,1,0:T(8,128)S(1)} %constant_dynamic-slice_fusion.2, ...), kind=kOutput, calls=%fused_computation.5.clone.1 | convolution fusion | flops 1074003968 | bytes 11010060 | tf_op jit(solution)/shard_map/while/body/dot_general | solution.py:32
  320.6 68.4 %reduce-scatter.2.cloned.1.call-done = f32[2,1,128,2048]{3,2,1,0:T(8,128)} async-done(((f32[8,1,128,2048]{3,2,1,0:T(8,128)}), f32[2,1,128,2048]{3,2,1,0:T(8,128)}) %reduce-scatter.2.cloned.1.call-update) | async-done | bytes 2097168 | tf_op jit(solution)/shard_map/reduce_scatter | solution.py:40
  389.0 2.7 convert_element_type.7
  (22 shorter events, 11.4 us)
Async XLA Ops:
  6.5 129.1 %all-gather.2.cloned.1.call-start = ((), (), s32[]{:S(2)}) async-start(), calls=%async_computation.1 | async-start | bytes 9437184 | tf_op jit(solution)/shard_map/all_gather | solution.py:10
  7.3 381.8 %reduce-scatter.2.cloned.1.call-start = ((), (), s32[]{:S(2)}) async-start(), calls=%async_computation.2 | async-start | bytes 10485760 | tf_op jit(solution)/shard_map/reduce_scatter | solution.py:40
Sparse Core Ops, SparseCore 0:
  9.5 126.1 all-gather.1
  320.7 68.2 reduce-scatter.1
where the time goes:
time: 403 us; the launch traced here: 399 us
  waiting for transfers between devices  196 us (49%)
  matrix products  89.9 us (22%)
  loops' own time  53.3 us (13%)
  local copies, waits for them, and re-layouts  41.7 us (10%)
  between operations  13.4 us (3%)
  other arithmetic  4.04 us (1%)
    all_gather x1, waiting for transfers between devices, body(): gathered = lax.all_gather(amplitudes, 'mem', axis=0, tiled=True)  127 us
    dot_general x12, matrix products, one_triple(): lax.dot_general(left, right, (((1,), (1,)), ((), ())), preferred_element_...  89.9 us
    reduce_scatter x1, waiting for transfers between devices, body(): lax.psum_scatter(partial_value.reshape(occ_tiles, ab_local, rows, width),...  68.4 us
    another operation x1, loops' own time, body(): partial_value = lax.fori_loop(0, live_count, one_triple, empty)  53.3 us
    dynamic_slice x12, local copies, waits for them, and re-layouts, one_triple(): current = lax.dynamic_index_in_dim(total, target_row, 0, keepdims=False)  15.6 us
  transfers between devices with their start and end apart: 2, of which 2 were waited for; matrix products, arithmetic and copies ran while one was open for 0% of the time, Pallas kernels for 0%

commit v1 on v0

--- a/solution.py
+++ b/solution.py
@@ -1,7 +1,241 @@
+import functools
+
 import jax
 import jax.numpy as jnp
 from jax import lax
+from jax.experimental import pallas as pl
+from jax.experimental.pallas import tpu as pltpu
 from jax.sharding import PartitionSpec as P
+
+MESH = pl.DeviceIdType.MESH
+LINE = 4
+HALVES = 2
+
+ORDERS = (
+    "0a 0b 1a 0A 1b 0B 2a 1A 2b 2A 3a 2B 3b 3A 3B 1B",
+    "1a 1b 2a 0a 1A 2b 0b 2A 3a 2B 3b 1B 3A 3B 0A 0B",
+    "2a 2b 3a 1a 2A 3b 1b 0a 3A 3B 0b 2B 1A 1B 0A 0B",
+    "3a 3b 2a 3A 2b 3B 1a 2A 1b 0a 1A 0b 1B 0A 2B 0B",
+)
+
+
+def entries(order):
+    return [(int(s[0]), int(s[1].isupper()), "ab".index(s[1].lower())) for s in order.split()]
+
+
+def tables():
+    out = []
+    for x in range(2):
+        for z in range(LINE):
+            steps = entries(ORDERS[z if x == 0 else LINE - 1 - z])
+            out.append([(sz if x == 0 else LINE - 1 - sz) * 4 + oy * 2 + h for sz, oy, h in steps])
+    return out
+
+
+def ladder_kernel(mask_ref, amp_ref, int_ref, out_ref, held, ints, part, near, far,
+                  load_sem, ints_sem, get_sem, up_sem, down_sem, side_sem,
+                  core_send, core_get, far_send, far_get):
+    grp, mem = lax.axis_index("grp"), lax.axis_index("mem")
+    x, core = grp // 2, grp % 2
+    z, y = mem // 2, mem % 2
+    up, down, side = {"mem": mem + 2}, {"mem": mem - 2}, {"mem": z * 2 + 1 - y}
+    pair_z = z + 1 - 2 * (z % 2)
+    pair = {"mem": pair_z * 2 + y}
+    twin = {"grp": x * 2 + 1 - core}
+    across = {"grp": (1 - x) * 2 + core}
+    width = ints.shape[1]
+    rows = held.shape[2]
+
+    load = pltpu.make_async_copy(amp_ref.at[0], held.at[mem], load_sem)
+    load.start()
+    fetch = [pltpu.make_async_copy(int_ref.at[0, h], ints.at[h], ints_sem.at[h]) for h in range(HALVES)]
+    for copy in fetch:
+        copy.start()
+
+    barrier = pltpu.get_barrier_semaphore()
+    for neighbour in (side, twin, across):
+        pl.semaphore_signal(barrier, inc=1, device_id=neighbour, device_id_type=MESH)
+
+    @pl.when(z < LINE - 1)
+    def _():
+        pl.semaphore_signal(barrier, inc=1, device_id=up, device_id_type=MESH)
+
+    @pl.when(z > 0)
+    def _():
+        pl.semaphore_signal(barrier, inc=1, device_id=down, device_id_type=MESH)
+
+    @pl.when((z > 0) & (z < LINE - 1))
+    def _():
+        pl.semaphore_wait(barrier, 5)
+
+    @pl.when((z == 0) | (z == LINE - 1))
+    def _():
+        pl.semaphore_wait(barrier, 4)
+
+    load.wait()
+
+    def push(tile, half, sems, target):
+        return pltpu.make_async_remote_copy(
+            src_ref=held.at[tile, half], dst_ref=held.at[tile, half],
+            send_sem=sems.at[tile, half], recv_sem=get_sem.at[tile, half],
+            device_id=target, device_id_type=MESH,
+        )
+
+    def pushes(sz, other, half, act):
+        tile = sz * 2 + y + other - 2 * y * other
+        same = other == 0
+
+        @pl.when(same & (sz <= z) & (z < LINE - 1))
+        def _():
+            act(push(tile, half, up_sem, up))
+
+        @pl.when(same & (sz >= z) & (z > 0))
+        def _():
+            act(push(tile, half, down_sem, down))
+
+        @pl.when(same & ((sz != pair_z) | (half == 0)))
+        def _():
+            act(push(tile, half, side_sem, side))
+
+        @pl.when((other == 1) & (sz == z) & (half == 1))
+        def _():
+            act(push(tile, half, up_sem, pair))
+
+    for half in range(HALVES):
+        pushes(z, 0, half, lambda copy: copy.start())
+
+    part[...] = jnp.zeros_like(part)
+    for copy in fetch:
+        copy.wait()
+
+    codes = tables()
+    words = []
+    for base in range(0, 16, 4):
+        word = jnp.int32(0)
+        for place, steps in enumerate(codes):
+            packed = sum(c << (4 * i) for i, c in enumerate(steps[base:base + 4]))
+            word = jnp.where(x * LINE + z == place, packed, word)
+        words.append(word)
+
+    def entry(step):
+        word = words[0]
+        for i in range(1, 4):
+            word = jnp.where(step // 4 == i, words[i], word)
+        shift = step % 4
+        scale = jnp.where(shift == 0, 1, jnp.where(shift == 1, 16, jnp.where(shift == 2, 256, 4096)))
+        code = word // scale % 16
+        return code // 4, code // 2 % 2, code % 2
+
+    def to_twin(tile):
+        place = tile // 4 * 2 + tile % 2
+        return pltpu.make_async_remote_copy(
+            src_ref=part.at[tile], dst_ref=near.at[place],
+            send_sem=core_send.at[place], recv_sem=core_get.at[place],
+            device_id=twin, device_id_type=MESH,
+        )
+
+    def to_across(tile):
+        place = tile % 2
+        return pltpu.make_async_remote_copy(
+            src_ref=part.at[tile], dst_ref=far.at[place],
+            send_sem=far_send.at[place], recv_sem=far_get.at[place],
+            device_id=across, device_id_type=MESH,
+        )
+
+    def one_step(step, carry):
+        sz, other, half = entry(step)
+        tile = sz * 2 + y + other - 2 * y * other
+
+        @pl.when(step >= HALVES)
+        def _():
+            push(tile, half, up_sem, pair).wait_recv()
+            pushes(sz, other, half, lambda copy: copy.start())
+
+        scale = mask_ref[tile * 2 + half]
+
+        def columns(n, inner):
+            at = pl.ds(pl.multiple_of(n * 512, 512), 512)
+            product = lax.dot_general(
+                held[tile, half], ints[half, at, :], (((1,), (1,)), ((), ())),
+                preferred_element_type=jnp.float32,
+            )
+            part[tile, :, at] += product * scale
+            return inner
+
+        lax.fori_loop(0, width // 512, columns, 0)
+        mine = tile // 2 % 2 == core
+
+        @pl.when((half == 1) & jnp.logical_not(mine))
+        def _():
+            to_twin(tile).start()
+
+        @pl.when((half == 1) & mine & (tile // 4 != x))
+        def _():
+            to_twin(tile).wait_recv()
+            part[tile] += near[tile // 4 * 2 + tile % 2]
+            to_across(tile).start()
+
+        return carry
+
+    lax.fori_loop(0, 16, one_step, 0)
+
+    for k in range(2):
+        tile = grp * 2 + k
+        to_twin(tile).wait_recv()
+        kept = part[tile] + near[x * 2 + k]
+        to_across(tile).wait_recv()
+        out_ref[k, 0] = (kept + far[k]).astype(out_ref.dtype)
+
+    def settle(step, carry):
+        sz, other, half = entry(step)
+        pushes(sz, other, half, lambda copy: copy.wait_send())
+        return carry
+
+    lax.fori_loop(0, 16, settle, 0)
+    for place in range(4):
+        tile = place // 2 * 4 + (1 - core) * 2 + place % 2
+        to_twin(tile).wait_send()
+    for k in range(2):
+        to_across((1 - x) * 4 + core * 2 + k).wait_send()
+
+
+def fused_body(amplitudes, integrals, triples):
+    rows, width = amplitudes.shape[2:]
+    codes = triples.reshape(-1)
+    tiles = 8
+    listed = (codes[None, :] == jnp.arange(tiles * HALVES, dtype=jnp.int32)[:, None]).any(axis=1)
+    flops = 2 * tiles * HALVES * rows * width * width
+    return pl.pallas_call(
+        ladder_kernel,
+        out_shape=jax.ShapeDtypeStruct((2, 1, rows, width), jnp.bfloat16),
+        in_specs=[
+            pl.BlockSpec(memory_space=pltpu.SMEM),
+            pl.BlockSpec(memory_space=pl.ANY),
+            pl.BlockSpec(memory_space=pl.ANY),
+        ],
+        out_specs=pl.BlockSpec(memory_space=pltpu.VMEM),
+        scratch_shapes=[
+            pltpu.VMEM((tiles, HALVES, rows, width), jnp.bfloat16),
+            pltpu.VMEM((HALVES, width, width), jnp.bfloat16),
+            pltpu.VMEM((tiles, rows, width), jnp.float32),
+            pltpu.VMEM((4, rows, width), jnp.float32),
+            pltpu.VMEM((2, rows, width), jnp.float32),
+            pltpu.SemaphoreType.DMA,
+            pltpu.SemaphoreType.DMA((HALVES,)),
+            pltpu.SemaphoreType.DMA((tiles, HALVES)),
+            pltpu.SemaphoreType.DMA((tiles, HALVES)),
+            pltpu.SemaphoreType.DMA((tiles, HALVES)),
+            pltpu.SemaphoreType.DMA((tiles, HALVES)),
+            pltpu.SemaphoreType.DMA((4,)),
+            pltpu.SemaphoreType.DMA((4,)),
+            pltpu.SemaphoreType.DMA((2,)),
+            pltpu.SemaphoreType.DMA((2,)),
+        ],
+        compiler_params=pltpu.CompilerParams(
+            collective_id=0, has_side_effects=True, vmem_limit_bytes=56 * 2**20,
+        ),
+        cost_estimate=pl.CostEstimate(flops=flops, bytes_accessed=18 * 2**20, transcendentals=0),
+    )(listed.astype(jnp.float32), amplitudes, integrals)
 
 
 def body(amplitudes, integrals, triples):
@@ -47,8 +281,9 @@
 
 
 def solution(mesh):
+    small = (mesh.shape["grp"], mesh.shape["mem"]) == (4, 8)
     return jax.shard_map(
-        body,
+        fused_body if small else body,
         mesh=mesh,
         in_specs=(P("mem", "grp", None, None), P("mem", "grp", None, None), P("grp", "mem", None)),
         out_specs=P("grp", "mem", None, None),

time: 403 us -> 120 us (0.30)
  the two profiles are of different devices: /device:TPU:2 before, /device:TPU:24 now
where the time goes in v1:
time: 120 us
  Pallas kernels  116 us (97%)
  local copies, waits for them, and re-layouts  2.3 us (2%)
  other arithmetic  1.29 us (1%)
    pallas_call x1, Pallas kernels, fused_body(): pl.pallas_call(ladder_kernel, out_shape=jax.ShapeDtypeStruct((2, 1, rows,...  116 us

profile of v1, /device:TPU:24, one launch (start us, length us, event | category | flops | bytes accessed | tf_op | source)
XLA Modules:
  0.0 119.8 jit_solution(13739446476895321625)
XLA Ops:
  0.0 0.8 fusion
  0.8 0.5 convert_element_type.3.mask_ref
  1.3 116.2 %shard_map.37 = bf16[2,1,128,2048]{3,2,1,0:T(8,128)(2,1)} custom-call(f32[16]{0:T(128)} %convert_element_type.3.mask_ref, bf16[1,2,128,2048]{3,2,1,0:T(8,128)(2,1)} %amp_ref.1, bf16[1,2,2048,2048]{3,2,1,0:T(8,128)(2,1)} %int_ref.1), custom_call_target="tpu_custom_call" | custom-call | flops 17179869184 | bytes 18874368 | tf_op jit(solution)/shard_map/pallas_call | solution.py:208
  117.5 2.3 %copy.5 = bf16[2,1,128,2048]{3,2,1,0:T(8,128)(2,1)} copy(bf16[2,1,128,2048]{3,2,1,0:T(8,128)(2,1)} %shard_map.37) | data formatting | bytes 2097152

commit v2 on v1

--- a/solution.py
+++ b/solution.py
@@ -10,26 +10,36 @@
 MESH = pl.DeviceIdType.MESH
 LINE = 4
 HALVES = 2
-
-ORDERS = (
-    "0a 0b 1a 0A 1b 0B 2a 1A 2b 2A 3a 2B 3b 3A 3B 1B",
-    "1a 1b 2a 0a 1A 2b 0b 2A 3a 2B 3b 1B 3A 3B 0A 0B",
-    "2a 2b 3a 1a 2A 3b 1b 0a 3A 3B 0b 2B 1A 1B 0A 0B",
-    "3a 3b 2a 3A 2b 3B 1a 2A 1b 0a 1A 0b 1B 0A 2B 0B",
+PARTS = 2
+
+FIRST_SENDS = 5
+MAIN_EVENTS = 114
+EVENTS = (
+    (
+        8700960, 25183331, 25446016, 2100386, 10093760, 35131911, 35784385, 4196391, 67208304, 29630981,
+        67471012, 4728976, 71404658, 30156309, 71667378, 6302868, 6169720, 47772185, 7418131, 73462810,
+        32257565, 73757800, 7918236, 8270858, 74273803, 3676350, 3939080, 45748876, 75645216, 75645216,
+        75645216, 75645216, 75645216, 75645216, 75645216, 75645216, 75645216, 75645216, 75645216,
+    ),
+    (
+        27824168, 28086825, 11341866, 3670186, 29401104, 69849288, 3932704, 29663761, 61182592, 8723723,
+        5244048, 29926418, 71426250, 5506594, 30189075, 63280802, 9266449, 5770388, 31502360, 71951552,
+        6565383, 35189337, 72214209, 7418038, 32027674, 73527490, 23868957, 27300987, 65373882, 19740953,
+        65551465, 25206042, 65895455, 25468699, 69325836, 61691917, 62392585, 42994432, 75629295,
+    ),
+    (
+        29925424, 30188081, 29402162, 21784208, 2188401, 54538262, 14296304, 2420824, 35664407, 72213201,
+        23359126, 2699385, 55063572, 23732466, 7088651, 63809194, 23947537, 7340218, 25182238, 73527510,
+        8141313, 33604129, 73790167, 621724, 25707524, 67237056, 9177603, 27283555, 65897122, 10815745,
+        50859113, 27809026, 51203079, 28071683, 69308428, 52762637, 52960521, 45621002, 75634379,
+    ),
+    (
+        23393368, 39892091, 4289627, 65069086, 4504858, 31515167, 74314384, 31768222, 65546258, 5515024,
+        71694002, 7351444, 6172926, 66939933, 96537, 25428576, 67111040, 1360898, 918148, 1655907, 27267330,
+        67980295, 35705353, 2756620, 36706922, 28055305, 69737642, 75586575, 75645216, 75645216, 75645216,
+        75645216, 75645216, 75645216, 75645216, 75645216, 75645216, 75645216, 75645195,
+    ),
 )
-
-
-def entries(order):
-    return [(int(s[0]), int(s[1].isupper()), "ab".index(s[1].lower())) for s in order.split()]
-
-
-def tables():
-    out = []
-    for x in range(2):
-        for z in range(LINE):
-            steps = entries(ORDERS[z if x == 0 else LINE - 1 - z])
-            out.append([(sz if x == 0 else LINE - 1 - sz) * 4 + oy * 2 + h for sz, oy, h in steps])
-    return out
 
 
 def ladder_kernel(mask_ref, amp_ref, int_ref, out_ref, held, ints, part, near, far,
@@ -38,9 +48,9 @@
     grp, mem = lax.axis_index("grp"), lax.axis_index("mem")
     x, core = grp // 2, grp % 2
     z, y = mem // 2, mem % 2
-    up, down, side = {"mem": mem + 2}, {"mem": mem - 2}, {"mem": z * 2 + 1 - y}
-    pair_z = z + 1 - 2 * (z % 2)
-    pair = {"mem": pair_z * 2 + y}
+    place_z = z + x * (LINE - 1 - 2 * z)
+    toward = 2 - 4 * x
+    up, down, side = {"mem": mem + toward}, {"mem": mem - toward}, {"mem": z * 2 + 1 - y}
     twin = {"grp": x * 2 + 1 - core}
     across = {"grp": (1 - x) * 2 + core}
     width = ints.shape[1]
@@ -56,11 +66,11 @@
     for neighbour in (side, twin, across):
         pl.semaphore_signal(barrier, inc=1, device_id=neighbour, device_id_type=MESH)
 
-    @pl.when(z < LINE - 1)
+    @pl.when(place_z < LINE - 1)
     def _():
         pl.semaphore_signal(barrier, inc=1, device_id=up, device_id_type=MESH)
 
-    @pl.when(z > 0)
+    @pl.when(place_z > 0)
     def _():
         pl.semaphore_signal(barrier, inc=1, device_id=down, device_id_type=MESH)
 
@@ -74,57 +84,36 @@
 
     load.wait()
 
-    def push(tile, half, sems, target):
+    share = rows // PARTS
+
+    def push(tile, half, piece, sems, target):
+        at = pl.ds(pl.multiple_of(piece * share, share), share)
         return pltpu.make_async_remote_copy(
-            src_ref=held.at[tile, half], dst_ref=held.at[tile, half],
-            send_sem=sems.at[tile, half], recv_sem=get_sem.at[tile, half],
+            src_ref=held.at[tile, half, at], dst_ref=held.at[tile, half, at],
+            send_sem=sems.at[tile, half * PARTS + piece], recv_sem=get_sem.at[tile, half * PARTS + piece],
             device_id=target, device_id_type=MESH,
         )
 
-    def pushes(sz, other, half, act):
+    words = []
+    for choices in zip(*EVENTS):
+        word = jnp.int32(choices[0])
+        for i in range(1, LINE):
+            word = jnp.where(place_z == i, choices[i], word)
+        words.append(word)
+
+    def event(step):
+        word = words[0]
+        for i in range(1, len(words)):
+            word = jnp.where(step // 3 == i, words[i], word)
+        third = step % 3
+        code = word // jnp.where(third == 0, 1, jnp.where(third == 1, 512, 512 * 512)) % 512
+        sz = code // 8 % 4
+        sz = sz + x * (LINE - 1 - 2 * sz)
+        other = code // 4 % 2
         tile = sz * 2 + y + other - 2 * y * other
-        same = other == 0
-
-        @pl.when(same & (sz <= z) & (z < LINE - 1))
-        def _():
-            act(push(tile, half, up_sem, up))
-
-        @pl.when(same & (sz >= z) & (z > 0))
-        def _():
-            act(push(tile, half, down_sem, down))
-
-        @pl.when(same & ((sz != pair_z) | (half == 0)))
-        def _():
-            act(push(tile, half, side_sem, side))
-
-        @pl.when((other == 1) & (sz == z) & (half == 1))
-        def _():
-            act(push(tile, half, up_sem, pair))
-
-    for half in range(HALVES):
-        pushes(z, 0, half, lambda copy: copy.start())
-
-    part[...] = jnp.zeros_like(part)
-    for copy in fetch:
-        copy.wait()
-
-    codes = tables()
-    words = []
-    for base in range(0, 16, 4):
-        word = jnp.int32(0)
-        for place, steps in enumerate(codes):
-            packed = sum(c << (4 * i) for i, c in enumerate(steps[base:base + 4]))
-            word = jnp.where(x * LINE + z == place, packed, word)
-        words.append(word)
-
-    def entry(step):
-        word = words[0]
-        for i in range(1, 4):
-            word = jnp.where(step // 4 == i, words[i], word)
-        shift = step % 4
-        scale = jnp.where(shift == 0, 1, jnp.where(shift == 1, 16, jnp.where(shift == 2, 256, 4096)))
-        code = word // scale % 16
-        return code // 4, code // 2 % 2, code % 2
+        return code // 32, tile, code // 2 % 2, code % 2
+
+    ways = ((up_sem, up), (down_sem, down), (side_sem, side))
 
     def to_twin(tile):
         place = tile // 4 * 2 + tile % 2
@@ -142,34 +131,47 @@
             device_id=across, device_id_type=MESH,
         )
 
-    def one_step(step, carry):
-        sz, other, half = entry(step)
-        tile = sz * 2 + y + other - 2 * y * other
-
-        @pl.when(step >= HALVES)
-        def _():
-            push(tile, half, up_sem, pair).wait_recv()
-            pushes(sz, other, half, lambda copy: copy.start())
-
+    def multiply(tile, half):
         scale = mask_ref[tile * 2 + half]
 
         def columns(n, inner):
             at = pl.ds(pl.multiple_of(n * 512, 512), 512)
             product = lax.dot_general(
-                held[tile, half], ints[half, at, :], (((1,), (1,)), ((), ())),
+                ints[half, at, :], held[tile, half], (((1,), (1,)), ((), ())),
                 preferred_element_type=jnp.float32,
             )
-            part[tile, :, at] += product * scale
+            part[tile, at, :] += product * scale
             return inner
 
         lax.fori_loop(0, width // 512, columns, 0)
+
+    def one_event(step, carry):
+        kind, tile, half, piece = event(step)
+
+        @pl.when(kind == 0)
+        def _():
+            push(tile, half, piece, side_sem, side).wait_recv()
+
+        for i, (sems, target) in enumerate(ways):
+            @pl.when(kind == 1 + i)
+            def _():
+                push(tile, half, piece, sems, target).start()
+
+            @pl.when(kind == 6 + i)
+            def _():
+                push(tile, half, piece, sems, target).wait_send()
+
+        @pl.when((kind == 4) | (kind == 5))
+        def _():
+            multiply(tile, half)
+
         mine = tile // 2 % 2 == core
 
-        @pl.when((half == 1) & jnp.logical_not(mine))
+        @pl.when((kind == 5) & jnp.logical_not(mine))
         def _():
             to_twin(tile).start()
 
-        @pl.when((half == 1) & mine & (tile // 4 != x))
+        @pl.when((kind == 5) & mine & (tile // 4 != x))
         def _():
             to_twin(tile).wait_recv()
             part[tile] += near[tile // 4 * 2 + tile % 2]
@@ -177,21 +179,21 @@
 
         return carry
 
-    lax.fori_loop(0, 16, one_step, 0)
+    lax.fori_loop(0, FIRST_SENDS, one_event, 0)
+    part[...] = jnp.zeros_like(part)
+    for copy in fetch:
+        copy.wait()
+
+    lax.fori_loop(FIRST_SENDS, MAIN_EVENTS, one_event, 0)
 
     for k in range(2):
         tile = grp * 2 + k
         to_twin(tile).wait_recv()
         kept = part[tile] + near[x * 2 + k]
         to_across(tile).wait_recv()
-        out_ref[k, 0] = (kept + far[k]).astype(out_ref.dtype)
-
-    def settle(step, carry):
-        sz, other, half = entry(step)
-        pushes(sz, other, half, lambda copy: copy.wait_send())
-        return carry
-
-    lax.fori_loop(0, 16, settle, 0)
+        out_ref[k, 0] = (kept + far[k]).T.astype(out_ref.dtype)
+
+    lax.fori_loop(MAIN_EVENTS, 3 * len(words), one_event, 0)
     for place in range(4):
         tile = place // 2 * 4 + (1 - core) * 2 + place % 2
         to_twin(tile).wait_send()
@@ -217,15 +219,15 @@
         scratch_shapes=[
             pltpu.VMEM((tiles, HALVES, rows, width), jnp.bfloat16),
             pltpu.VMEM((HALVES, width, width), jnp.bfloat16),
-            pltpu.VMEM((tiles, rows, width), jnp.float32),
-            pltpu.VMEM((4, rows, width), jnp.float32),
-            pltpu.VMEM((2, rows, width), jnp.float32),
+            pltpu.VMEM((tiles, width, rows), jnp.float32),
+            pltpu.VMEM((4, width, rows), jnp.float32),
+            pltpu.VMEM((2, width, rows), jnp.float32),
             pltpu.SemaphoreType.DMA,
             pltpu.SemaphoreType.DMA((HALVES,)),
-            pltpu.SemaphoreType.DMA((tiles, HALVES)),
-            pltpu.SemaphoreType.DMA((tiles, HALVES)),
-            pltpu.SemaphoreType.DMA((tiles, HALVES)),
-            pltpu.SemaphoreType.DMA((tiles, HALVES)),
+            pltpu.SemaphoreType.DMA((tiles, HALVES * PARTS)),
+            pltpu.SemaphoreType.DMA((tiles, HALVES * PARTS)),
+            pltpu.SemaphoreType.DMA((tiles, HALVES * PARTS)),
+            pltpu.SemaphoreType.DMA((tiles, HALVES * PARTS)),
             pltpu.SemaphoreType.DMA((4,)),
             pltpu.SemaphoreType.DMA((4,)),
             pltpu.SemaphoreType.DMA((2,)),

time: 120 us -> 115 us (0.958)
  the two profiles are of different devices: /device:TPU:24 before, /device:TPU:2 now
where the time goes in v2:
time: 115 us
  Pallas kernels  111 us (97%)
  local copies, waits for them, and re-layouts  2.3 us (2%)
  other arithmetic  1.29 us (1%)
    pallas_call x1, Pallas kernels, fused_body(): pl.pallas_call(ladder_kernel, out_shape=jax.ShapeDtypeStruct((2, 1, rows,...  111 us
    unnamed x1, local copies, waits for them, and re-layouts  2.3 us

profile of v2, /device:TPU:2, one launch (start us, length us, event | category | flops | bytes accessed | tf_op | source)
XLA Modules:
  0.0 114.6 jit_solution(16585521456271635840)
XLA Ops:
  0.0 0.8 fusion
  0.8 0.5 convert_element_type.3.mask_ref
  1.3 110.9 %shard_map.37 = bf16[2,1,128,2048]{3,2,1,0:T(8,128)(2,1)} custom-call(f32[16]{0:T(128)} %convert_element_type.3.mask_ref, bf16[1,2,128,2048]{3,2,1,0:T(8,128)(2,1)} %amp_ref.1, bf16[1,2,2048,2048]{3,2,1,0:T(8,128)(2,1)} %int_ref.1), custom_call_target="tpu_custom_call" | custom-call | flops 17179869184 | bytes 18874368 | tf_op jit(solution)/shard_map/pallas_call | solution.py:210
  112.2 2.3 %copy.5 = bf16[2,1,128,2048]{3,2,1,0:T(8,128)(2,1)} copy(bf16[2,1,128,2048]{3,2,1,0:T(8,128)(2,1)} %shard_map.37) | data formatting | bytes 2097152

commit v3 on v2

--- a/solution.py
+++ b/solution.py
@@ -12,29 +12,29 @@
 HALVES = 2
 PARTS = 2
 
-FIRST_SENDS = 5
+FIRST_SENDS = 6
 MAIN_EVENTS = 114
 EVENTS = (
     (
-        8700960, 25183331, 25446016, 2100386, 10093760, 35131911, 35784385, 4196391, 67208304, 29630981,
+        8700960, 25183331, 33604131, 9965574, 67731618, 10228231, 67994246, 4196488, 67208304, 29630981,
         67471012, 4728976, 71404658, 30156309, 71667378, 6302868, 6169720, 47772185, 7418131, 73462810,
-        32257565, 73757800, 7918236, 8270858, 74273803, 3676350, 3939080, 45748876, 75645216, 75645216,
+        32257565, 48812648, 7944473, 8270858, 74273803, 3676350, 3939080, 45748876, 75645216, 75645216,
         75645216, 75645216, 75645216, 75645216, 75645216, 75645216, 75645216, 75645216, 75645216,
     ),
     (
-        27824168, 28086825, 11341866, 3670186, 29401104, 69849288, 3932704, 29663761, 61182592, 8723723,
-        5244048, 29926418, 71426250, 5506594, 30189075, 63280802, 9266449, 5770388, 31502360, 71951552,
-        6565383, 35189337, 72214209, 7418038, 32027674, 73527490, 23868957, 27300987, 65373882, 19740953,
-        65551465, 25206042, 65895455, 25468699, 69325836, 61691917, 62392585, 42994432, 75629295,
-    ),
-    (
-        29925424, 30188081, 29402162, 21784208, 2188401, 54538262, 14296304, 2420824, 35664407, 72213201,
-        23359126, 2699385, 55063572, 23732466, 7088651, 63809194, 23947537, 7340218, 25182238, 73527510,
-        8141313, 33604129, 73790167, 621724, 25707524, 67237056, 9177603, 27283555, 65897122, 10815745,
-        50859113, 27809026, 51203079, 28071683, 69308428, 52762637, 52960521, 45621002, 75634379,
-    ),
-    (
-        23393368, 39892091, 4289627, 65069086, 4504858, 31515167, 74314384, 31768222, 65546258, 5515024,
+        27824168, 28086825, 35673642, 4201472, 29401120, 60919978, 3932938, 21250577, 52756593, 37361385,
+        4728834, 29926434, 71426250, 5506704, 21775891, 53298291, 46801649, 6302726, 50393176, 38937842,
+        6565383, 35189337, 72214209, 6830262, 50918490, 39989496, 23868957, 27300987, 48812619, 73790147,
+        25205916, 74052638, 8176207, 74315454, 69325836, 61691917, 62392585, 42994432, 75629295,
+    ),
+    (
+        29925424, 30188081, 29402162, 29664819, 5771408, 23096344, 54617208, 2499824, 14430743, 35713625,
+        72213201, 5248150, 55096346, 39985394, 7088651, 55399515, 47325939, 7878656, 56148000, 48902392,
+        8141313, 33604129, 73790167, 1049756, 50381858, 49938682, 9177603, 27283555, 42521129, 67499713,
+        27808900, 67732486, 1889835, 67995302, 69308428, 52762637, 52960521, 45621002, 75634379,
+    ),
+    (
+        23393368, 23901307, 7872664, 48816222, 4601080, 29670943, 37810808, 41563897, 65546258, 5515024,
         71694002, 7351444, 6172926, 66939933, 96537, 25428576, 67111040, 1360898, 918148, 1655907, 27267330,
         67980295, 35705353, 2756620, 36706922, 28055305, 69737642, 75586575, 75645216, 75645216, 75645216,
         75645216, 75645216, 75645216, 75645216, 75645216, 75645216, 75645216, 75645195,

time: 115 us -> 114 us (level)
  no operation moved by 1% of the time
where the time goes in v3:
time: 114 us; the launch traced here: 113 us
  Pallas kernels  110 us (96%)
  local copies, waits for them, and re-layouts  2.3 us (2%)
  other arithmetic  1.29 us (1%)
    pallas_call x1, Pallas kernels, fused_body(): pl.pallas_call(ladder_kernel, out_shape=jax.ShapeDtypeStruct((2, 1, rows,...  110 us
    unnamed x1, local copies, waits for them, and re-layouts  2.3 us

profile of v3, /device:TPU:2, one launch (start us, length us, event | category | flops | bytes accessed | tf_op | source)
XLA Modules:
  0.0 113.4 jit_solution(2116494619701225533)
XLA Ops:
  0.0 0.8 fusion
  0.8 0.5 convert_element_type.3.mask_ref
  1.3 109.8 %shard_map.37 = bf16[2,1,128,2048]{3,2,1,0:T(8,128)(2,1)} custom-call(f32[16]{0:T(128)} %convert_element_type.3.mask_ref, bf16[1,2,128,2048]{3,2,1,0:T(8,128)(2,1)} %amp_ref.1, bf16[1,2,2048,2048]{3,2,1,0:T(8,128)(2,1)} %int_ref.1), custom_call_target="tpu_custom_call" | custom-call | flops 17179869184 | bytes 18874368 | tf_op jit(solution)/shard_map/pallas_call | solution.py:210
  111.1 2.3 %copy.5 = bf16[2,1,128,2048]{3,2,1,0:T(8,128)(2,1)} copy(bf16[2,1,128,2048]{3,2,1,0:T(8,128)(2,1)} %shard_map.37) | data formatting | bytes 2097152
